TPU v7x, 32 devices: a whole 2x2x4 slice. The times are simulated.
32 devices in a mesh: variant: 2 (over y), row: 4 (over z), col: 2 (over x), sub: 2 (over core).
Axes of the slice: x: 2, y: 2, z: 4, core: 2. Of those that a mesh axis runs over, the one named last changes fastest.
Arguments:
- charges: bfloat16 [512, 128, 128], P(('variant', 'row', 'col', 'sub')), parts along dimension 0, may hold values from -6 to 6
- adj_loads: bfloat16 [512, 128, 128], P(('variant', 'row', 'col', 'sub')), parts along dimension 0, may hold values from -6 to 6
- bases: bfloat16 [512, 32, 128], P(('variant', 'row', 'col', 'sub')), parts along dimension 0, may hold values from -0.5 to 0.5
- couplings: bfloat16 [8192, 1024], P(('variant', 'row', 'col', 'sub')), parts along dimension 0, may hold values from -0.25 to 0.25
- near_blocks: bfloat16 [1536, 128, 128], P(('variant', 'row', 'col', 'sub')), parts along dimension 0, may hold values from -0.3125 to 0.3125
- near_rows: int32 [16, 48], P(('row', 'col', 'sub')), may hold values from 0 to 31
- near_cols: int32 [16, 48], P(('row', 'col', 'sub')), may hold values from 0 to 15
- far_rows: int32 [16, 256], P(('row', 'col', 'sub')), may hold values from 0 to 15
- far_slots: int32 [16, 256], P(('row', 'col', 'sub')), may hold values from 0 to 15, as said below
- send_list: int32 [16, 8, 2], P(('row', 'col', 'sub')), may hold values from -1 to 15, as said below
Outputs:
- potentials: bfloat16 [512, 128, 128], P(('variant', 'row', 'col', 'sub')), parts along dimension 0
- adjoint_field: bfloat16 [512, 128, 128], P(('variant', 'row', 'col', 'sub')), parts along dimension 0
There are 2 independent parts, one for each index of `variant`. A program takes and returns all parts, laid end to end along the dimension named above; an argument that names none is the same for every part. Nothing has to cross between parts.
Inputs may be any that keep to these rules, and one draw needn't show every extreme that they name: `send_list`: entry [o, p, k] is a cluster of owner o, numbered within that owner, or -1 for an empty slot; the live slots of each [o, p] come first; for each draw some peer p receives 2 live slots from every owner. `far_slots`: A far pair names slot (p, k) of its owner as p * 2 + k; the slot is live in the send_list of owner p * 2 + o % 2, and every live slot of the owner is named by one far pair or more.
All inputs are finite; a program needn't handle non-finite values.
Results may differ from a plain program's by a relative error of at most 0.005.
Values may be sent and summed in bfloat16 or wider, within the bound.
A program may use at most 384 MiB of HBM per device.

v0:
```python
import jax
import jax.numpy as jnp
from jax import lax
from jax.sharding import PartitionSpec as P

highest = lax.Precision.HIGHEST


def move_slots(payload):
    result = lax.all_to_all(
        payload.astype(jnp.bfloat16), ("row", "col"), split_axis=0, concat_axis=0, tiled=True
    ).astype(payload.dtype)
    return result


def on_device(
    charges,
    adj_loads,
    bases,
    couplings,
    near_blocks,
    near_rows,
    near_cols,
    far_rows,
    far_slots,
    send_list,
):
    clusters = charges.shape[0]
    block_size = charges.shape[1]
    load_count = charges.shape[2]
    rank_dim = bases.shape[1]
    peer_count = send_list.shape[1]
    capacity = send_list.shape[2]
    total_slots = peer_count * capacity
    coeffs = jnp.einsum("ckb,cbr->ckr", bases, charges, preferred_element_type=jnp.float32).astype(
        jnp.bfloat16
    )
    adj_coeffs = jnp.einsum(
        "ckb,cbr->ckr", bases, adj_loads, preferred_element_type=jnp.float32
    ).astype(jnp.bfloat16)
    send_ids = send_list[0].reshape(total_slots)
    cluster_ids = jnp.arange(clusters, dtype=jnp.int32)
    slot_onehot = (send_ids[None, :] == cluster_ids[:, None]).astype(jnp.float32)
    outgoing = jnp.einsum("ct,ckr->tkr", slot_onehot, coeffs.astype(jnp.float32), precision=highest)
    outgoing = outgoing.reshape(peer_count, capacity, rank_dim, load_count)
    coupling_mats = couplings.reshape(-1, rank_dim, rank_dim).astype(jnp.float32)
    pair_slots = far_slots[0]
    pair_rows = far_rows[0]
    merged = jnp.zeros((clusters * total_slots, rank_dim, rank_dim), jnp.float32)
    merged = merged.at[pair_rows * total_slots + pair_slots].add(coupling_mats)
    merged = merged.reshape(clusters, total_slots, rank_dim, rank_dim).transpose(0, 2, 1, 3)
    merged = merged.reshape(clusters * rank_dim, total_slots * rank_dim)
    adj_flat = adj_coeffs.astype(jnp.float32).reshape(clusters * rank_dim, load_count)
    returns_out = jnp.dot(merged.T, adj_flat, precision=highest)
    returns_out = returns_out.reshape(peer_count, capacity, rank_dim, load_count)
    arrived = move_slots(outgoing)
    returned = move_slots(returns_out)
    arrived_flat = (
        arrived.reshape(total_slots * rank_dim, load_count).astype(jnp.bfloat16).astype(jnp.float32)
    )
    far_fwd = jnp.dot(merged, arrived_flat, precision=highest).reshape(
        clusters, rank_dim, load_count
    )
    far_adj = jnp.einsum(
        "ct,tkr->ckr",
        slot_onehot,
        returned.reshape(total_slots, rank_dim, load_count),
        precision=highest,
    )
    sub_size = lax.axis_size("sub")
    block_rows = near_rows[0]
    block_cols = near_cols[0]
    row_onehot = (
        block_rows[:, None] == jnp.arange(sub_size * clusters, dtype=jnp.int32)[None, :]
    ).astype(jnp.float32)
    col_onehot = (block_cols[:, None] == cluster_ids[None, :]).astype(jnp.float32)
    near_terms = jnp.einsum(
        "nij,njr->nir", near_blocks, charges[block_cols], preferred_element_type=jnp.float32
    )
    near_partial = jnp.dot(
        row_onehot.T, near_terms.reshape(-1, block_size * load_count), precision=highest
    )
    near_partial = near_partial.reshape(sub_size * clusters, block_size, load_count)
    near_fwd = lax.psum_scatter(near_partial, "sub", scatter_dimension=0, tiled=True)
    chip_loads = lax.all_gather(adj_loads, "sub", axis=0, tiled=True)
    near_back = jnp.einsum(
        "nij,nir->njr", near_blocks, chip_loads[block_rows], preferred_element_type=jnp.float32
    )
    near_adj = jnp.dot(
        col_onehot.T, near_back.reshape(-1, block_size * load_count), precision=highest
    )
    near_adj = near_adj.reshape(clusters, block_size, load_count)
    base32 = bases.astype(jnp.float32)
    potentials = jnp.einsum("ckb,ckr->cbr", base32, far_fwd, precision=highest) + near_fwd
    adjoint_field = jnp.einsum("ckb,ckr->cbr", base32, far_adj, precision=highest) + near_adj
    return (potentials.astype(jnp.bfloat16), adjoint_field.astype(jnp.bfloat16))


def solution(mesh):
    in_specs = (
        P(("variant", "row", "col", "sub"), None, None),
        P(("variant", "row", "col", "sub"), None, None),
        P(("variant", "row", "col", "sub"), None, None),
        P(("variant", "row", "col", "sub"), None),
        P(("variant", "row", "col", "sub"), None, None),
        P(("row", "col", "sub"), None),
        P(("row", "col", "sub"), None),
        P(("row", "col", "sub"), None),
        P(("row", "col", "sub"), None),
        P(("row", "col", "sub"), None, None),
    )
    out_specs = (
        P(("variant", "row", "col", "sub"), None, None),
        P(("variant", "row", "col", "sub"), None, None),
    )
    return jax.shard_map(
        on_device, mesh=mesh, in_specs=in_specs, out_specs=out_specs, check_vma=False
    )
```

profile of v0, /device:TPU:0, one launch (start us, length us, event | category | flops | bytes accessed | tf_op | source)
XLA Modules:
  0.0 136.6 jit_solution(11950972633794787091)
XLA Ops:
  8.6 1.9 %gather_fusion = bf16[48,128,128]{2,1,0:T(8,128)(2,1)S(1)} fusion(bf16[16,128,128]{2,1,0:T(8,128)(2,1)} %param.10, s32[1024]{0:T(1024)S(1)} %pad_clamp_fusion.1), kind=kCustom, calls=%fused_computation | custom fusion | bytes 3145920 | tf_op jit(solution)/shard_map/gather | solution.py:78
  10.5 2.9 %convolution_bitcast_fusion.1 = f32[48,128,128]{1,2,0:T(8,128)} fusion(bf16[48,128,128]{2,1,0:T(8,128)(2,1)S(1)} %gather_fusion, bf16[48,128,128]{2,1,0:T(8,128)(2,1)S(1)} %copy-done), kind=kOutput, calls=%fused_computation.12 | convolution fusion | flops 201326592 | bytes 6291456 | tf_op jit(solution)/shard_map/nij,njr->nir/dot_general | solution.py:77
  13.5 3.5 %copy.82 = f32[48,128,128]{2,1,0:T(8,128)} copy(f32[48,128,128]{1,2,0:T(8,128)} %convolution_bitcast_fusion.1) | data formatting | bytes 6291456 | tf_op jit(solution)/shard_map/nij,njr->nir/dot_general | solution.py:77
  17.0 6.5 %fusion.3 = f32[32,128,128]{2,0,1:T(8,128)} fusion(s32[48]{0:T(128)S(1)} %bitcast.114, f32[6,8,128,128]{3,2,1,0:T(8,128)} %bitcast.104), kind=kOutput, calls=%fused_computation.8 | convolution fusion | flops 301991424 | bytes 5243072 | tf_op jit(solution)/shard_map/dot_general | solution.py:80
  23.5 3.0 %copy.84 = f32[32,128,128]{1,2,0:T(8,128)} copy(f32[32,128,128]{2,0,1:T(8,128)} %fusion.3) | data formatting | bytes 4194304 | tf_op jit(solution)/shard_map/dot_general | solution.py:80
  26.8 3.8 %copy.75 = f32[256,32,32]{2,1,0:T(8,128)} copy(bf16[256,32,32]{0,2,1:T(8,128)(2,1)S(1)} %bitcast.107) | data formatting | bytes 1572864 | tf_op jit(solution)/shard_map/convert_element_type | solution.py:46
  30.6 2.5 %broadcast_in_dim.2 = f32[256,32,32]{2,1,0:T(8,128)} broadcast(f32[]{:T(128)} %constant.5.clone.1), dimensions={} | broadcast | bytes 1048580 | tf_op jit(solution)/shard_map/broadcast_in_dim | solution.py:49
  33.1 34.1 %scatter_fusion = f32[256,32,32]{2,1,0:T(8,128)} fusion(f32[256,32,32]{2,1,0:T(8,128)} %broadcast_in_dim.2, s32[256]{0:T(256)S(1)} %bitcast.112, f32[256,32,32]{2,1,0:T(8,128)} %copy.75), kind=kCustom, calls=%fused_computation.2 | custom fusion | flops 262144 | bytes 3146752 | tf_op jit(solution)/shard_map/scatter-add | solution.py:50
  67.1 7.4 %copy.76 = f32[16,32,16,32]{3,2,1,0:T(8,128)} copy(f32[16,32,16,32]{3,1,2,0:T(8,128)} %bitcast.102) | data formatting | bytes 2097152 | tf_op jit(solution)/shard_map/transpose | solution.py:51
  74.6 3.6 %reshape.131 = f32[512,512]{1,0:T(8,128)S(1)} reshape(f32[16,32,16,32]{3,2,1,0:T(8,128)} %copy.76) | data formatting | bytes 2097152 | tf_op jit(solution)/shard_map/reshape | solution.py:52
  78.2 1.3 copy.86
  79.8 2.5 %convolution_convert_fusion.2 = bf16[8,2,32,128]{3,2,1,0:T(8,128)(2,1)} fusion(f32[8,2,32,512]{3,2,1,0:T(8,128)} %bitcast.106, bf16[512,128,1,1]{1,0,3,2:T(8,128)(2,1)S(1)} %bitcast.109), kind=kOutput, calls=%fused_computation.21 | convolution fusion | flops 402718720 | bytes 1310720 | tf_op jit(solution)/shard_map/dot_general | solution.py:54
  82.3 7.3 %all-to-all-start.1 = ((bf16[8,2,32,128]{3,2,1,0:T(8,128)(2,1)}), bf16[8,2,32,128]{3,2,1,0:T(8,128)(2,1)S(1)}, u32[]{:S(2)}, u32[]{:S(2)}) async-start(bf16[8,2,32,128]{3,2,1,0:T(8,128)(2,1)} %convolution_convert_fusion.2), calls=%async_computation.2 | async-start | bytes 262144 | tf_op jit(solution)/shard_map/all_to_all | solution.py:10
  89.6 3.5 %dot_general.58 = f32[16,32,512]{2,1,0:T(8,128)S(1)} reshape(f32[16,32,16,32]{3,2,1,0:T(8,128)} %copy.76) | data formatting | bytes 2097152 | tf_op jit(solution)/shard_map/dot_general | solution.py:61
  94.5 2.4 %all-to-all-done.1 = bf16[8,2,32,128]{3,2,1,0:T(8,128)(2,1)S(1)} async-done(((bf16[8,2,32,128]{3,2,1,0:T(8,128)(2,1)}), bf16[8,2,32,128]{3,2,1,0:T(8,128)(2,1)S(1)}, u32[]{:S(2)}, u32[]{:S(2)}) %all-to-all-start.1) | async-done | bytes 131104 | tf_op jit(solution)/shard_map/all_to_all | solution.py:10
  96.9 3.6 %all-to-all-start = ((bf16[8,2,32,128]{3,2,1,0:T(8,128)(2,1)}), bf16[8,2,32,128]{3,2,1,0:T(8,128)(2,1)S(1)}, u32[]{:S(2)}, u32[]{:S(2)}) async-start(bf16[8,2,32,128]{3,2,1,0:T(8,128)(2,1)} %copy.80), calls=%async_computation | async-start | bytes 262144 | tf_op jit(solution)/shard_map/all_to_all | solution.py:10
  101.6 6.3 %all-to-all-done = bf16[8,2,32,128]{3,2,1,0:T(8,128)(2,1)S(1)} async-done(((bf16[8,2,32,128]{3,2,1,0:T(8,128)(2,1)}), bf16[8,2,32,128]{3,2,1,0:T(8,128)(2,1)S(1)}, u32[]{:S(2)}, u32[]{:S(2)}) %all-to-all-start) | async-done | bytes 131104 | tf_op jit(solution)/shard_map/all_to_all | solution.py:10
  109.2 2.1 %gather_fusion.1 = bf16[48,128,128]{2,1,0:T(8,128)(2,1)S(1)} fusion(bf16[32,128,128]{2,1,0:T(8,128)(2,1)} %all-gather.2.cloned.1.call-done, s32[1024]{0:T(1024)S(1)} %pad_clamp_fusion), kind=kCustom, calls=%fused_computation.1 | custom fusion | bytes 3145920 | tf_op jit(solution)/shard_map/gather | solution.py:87
  111.3 2.3 %convolution_bitcast_fusion = f32[48,128,128]{1,2,0:T(8,128)} fusion(bf16[48,128,128]{2,1,0:T(8,128)(2,1)S(1)} %gather_fusion.1, bf16[48,128,128]{2,1,0:T(8,128)(2,1)S(1)} %copy-done), kind=kOutput, calls=%fused_computation.11 | convolution fusion | flops 201326592 | bytes 6291456 | tf_op jit(solution)/shard_map/nij,nir->njr/dot_general | solution.py:86
  113.6 3.6 %copy.90 = f32[48,128,128]{2,1,0:T(8,128)} copy(f32[48,128,128]{1,2,0:T(8,128)} %convolution_bitcast_fusion) | data formatting | bytes 6291456 | tf_op jit(solution)/shard_map/nij,nir->njr/dot_general | solution.py:86
  117.2 4.6 %fusion = f32[16,128,128]{2,0,1:T(8,128)S(1)} fusion(s32[48]{0:T(128)S(1)} %bitcast.113, f32[6,8,128,128]{3,2,1,0:T(8,128)} %bitcast.103), kind=kOutput, calls=%fused_computation.5 | convolution fusion | flops 150995712 | bytes 4194496 | tf_op jit(solution)/shard_map/dot_general | solution.py:89
  121.9 1.4 %copy.92 = f32[16,128,128]{1,2,0:T(8,128)} copy(f32[16,128,128]{2,0,1:T(8,128)S(1)} %fusion) | data formatting | bytes 2097152 | tf_op jit(solution)/shard_map/dot_general | solution.py:89
  123.3 2.2 %fusion.8 = bf16[16,128,128]{1,2,0:T(8,128)(2,1)S(1)} fusion(f32[16,128,128]{1,2,0:T(8,128)} %copy.92, bf16[16,32,128]{2,1,0:T(8,128)(2,1)S(1)} %copy-done.3, f32[16,32,128]{2,0,1:T(8,128)S(1)} %fusion.11), kind=kOutput, calls=%fused_computation.17 | convolution fusion | flops 101187584 | bytes 1966080 | tf_op jit(solution)/shard_map/ckb,ckr->cbr/dot_general | solution.py:95
  126.5 2.2 %fusion.9 = bf16[16,128,128]{1,2,0:T(8,128)(2,1)S(1)} fusion(f32[16,128,128]{1,2,0:T(8,128)} %reduce-scatter.2.cloned.1.call-done, f32[16,32,128]{2,1,0:T(8,128)S(1)} %copy-done.4, bf16[16,32,128]{2,1,0:T(8,128)(2,1)S(1)} %copy-done.3), kind=kOutput, calls=%fused_computation.18 | convolution fusion | flops 101187584 | bytes 1966080 | tf_op jit(solution)/shard_map/ckb,ckr->cbr/dot_general | solution.py:94
  (46 shorter events, 7.7 us)
Async XLA Ops:
  7.2 3.4 %copy-start = (bf16[48,128,128]{2,1,0:T(8,128)(2,1)S(1)}, bf16[48,128,128]{2,1,0:T(8,128)(2,1)}, u32[]{:S(2)}) copy-start(bf16[48,128,128]{2,1,0:T(8,128)(2,1)} %param.14) | copy-start | bytes 4718596
  7.2 102.0 %all-gather.2.cloned.1.call-start = ((), (), s32[]{:S(2)}) async-start(), calls=%async_computation.4 | async-start | bytes 1572864 | tf_op jit(solution)/shard_map/all_gather | solution.py:85
  7.9 118.6 %reduce-scatter.2.cloned.1.call-start = ((), (), s32[]{:S(2)}) async-start(), calls=%async_computation.3 | async-start | bytes 3145728 | tf_op jit(solution)/shard_map/reduce_scatter | solution.py:84
  13.5 3.6 %copy-start.11 = (s32[1,48]{1,0:T(1,128)S(1)}, s32[1,48]{1,0:T(1,128)}, u32[]{:S(2)}) copy-start(s32[1,48]{1,0:T(1,128)} %param.15) | copy-start | bytes 580
  23.5 3.1 %copy-start.5 = (bf16[256,1024]{1,0:T(8,128)(2,1)S(1)}, bf16[256,1024]{1,0:T(8,128)(2,1)}, u32[]{:S(2)}) copy-start(bf16[256,1024]{1,0:T(8,128)(2,1)} %param.13) | copy-start | bytes 1572868
  26.6 4.0 %copy-start.7 = (s32[1,256]{1,0:T(1,128)S(1)}, s32[1,256]{1,0:T(1,128)}, u32[]{:S(2)}) copy-start(s32[1,256]{1,0:T(1,128)} %param.18) | copy-start | bytes 3076
  26.6 4.0 %copy-start.8 = (s32[1,256]{1,0:T(1,128)S(1)}, s32[1,256]{1,0:T(1,128)}, u32[]{:S(2)}) copy-start(s32[1,256]{1,0:T(1,128)} %param.17) | copy-start | bytes 3076
  74.5 5.0 %copy-start.2 = (bf16[16,128,128]{2,1,0:T(8,128)(2,1)S(1)}, bf16[16,128,128]{2,1,0:T(8,128)(2,1)}, u32[]{:S(2)}) copy-start(bf16[16,128,128]{2,1,0:T(8,128)(2,1)} %param.11) | copy-start | bytes 1572868
  74.5 5.0 %copy-start.3 = (bf16[16,32,128]{2,1,0:T(8,128)(2,1)S(1)}, bf16[16,32,128]{2,1,0:T(8,128)(2,1)}, u32[]{:S(2)}) copy-start(bf16[16,32,128]{2,1,0:T(8,128)(2,1)} %param.12) | copy-start | bytes 393220
  79.7 13.4 %copy-start.9 = (s32[1,8,2]{1,2,0:T(2,128)S(1)}, s32[1,8,2]{1,2,0:T(2,128)}, u32[]{:S(2)}) copy-start(s32[1,8,2]{1,2,0:T(2,128)} %param.19) | copy-start | bytes 196
  79.7 13.6 %copy-start.1 = (bf16[16,128,128]{2,1,0:T(8,128)(2,1)S(1)}, bf16[16,128,128]{2,1,0:T(8,128)(2,1)}, u32[]{:S(2)}) copy-start(bf16[16,128,128]{2,1,0:T(8,128)(2,1)} %param.10) | copy-start | bytes 1572868
  82.3 14.6 %all-to-all-start.1 = ((bf16[8,2,32,128]{3,2,1,0:T(8,128)(2,1)}), bf16[8,2,32,128]{3,2,1,0:T(8,128)(2,1)S(1)}, u32[]{:S(2)}, u32[]{:S(2)}) async-start(bf16[8,2,32,128]{3,2,1,0:T(8,128)(2,1)} %convolution_convert_fusion.2), calls=%async_computation.2 | async-start | bytes 262144 | tf_op jit(solution)/shard_map/all_to_all | solution.py:10
  96.9 3.6 %copy-start.6 = (bf16[8,2,32,128]{3,2,1,0:T(8,128)(2,1)}, bf16[8,2,32,128]{3,2,1,0:T(8,128)(2,1)S(1)}, u32[]{:S(2)}) copy-start(bf16[8,2,32,128]{3,2,1,0:T(8,128)(2,1)S(1)} %all-to-all-done.1) | copy-start | bytes 393220
  96.9 11.0 %all-to-all-start = ((bf16[8,2,32,128]{3,2,1,0:T(8,128)(2,1)}), bf16[8,2,32,128]{3,2,1,0:T(8,128)(2,1)S(1)}, u32[]{:S(2)}, u32[]{:S(2)}) async-start(bf16[8,2,32,128]{3,2,1,0:T(8,128)(2,1)} %copy.80), calls=%async_computation | async-start | bytes 262144 | tf_op jit(solution)/shard_map/all_to_all | solution.py:10
  113.6 3.6 %copy-start.10 = (s32[1,48]{1,0:T(1,128)S(1)}, s32[1,48]{1,0:T(1,128)}, u32[]{:S(2)}) copy-start(s32[1,48]{1,0:T(1,128)} %param.16) | copy-start | bytes 580
  121.8 4.7 %copy-start.4 = (f32[16,32,128]{2,1,0:T(8,128)S(1)}, f32[16,32,128]{2,1,0:T(8,128)}, u32[]{:S(2)}) copy-start(f32[16,32,128]{2,1,0:T(8,128)} %fusion.27) | copy-start | bytes 786436
Sparse Core Ops, SparseCore 0:
  9.6 11.7 all-gather.1
  26.7 12.2 reduce-scatter.1
where the time goes:
time: 138 us; the launch traced here: 137 us
  local copies, waits for them, and re-layouts  40.8 us (30%)
  other arithmetic  34.7 us (25%)
  matrix products  26.5 us (19%)
  between operations  14.2 us (10%)
  starting transfers between devices  11 us (8%)
  waiting for transfers between devices  9.38 us (7%)
    scatter-add x1, other arithmetic, on_device(): merged = merged.at[pair_rows * total_slots + pair_slots].add(coupling_mats)  34.1 us
    all_to_all x2, starting transfers between devices, move_slots(): lax.all_to_all(payload.astype(jnp.bfloat16), ('row', 'col'), split_axis=0...  10.9 us
    all_to_all x2, waiting for transfers between devices, move_slots(): lax.all_to_all(payload.astype(jnp.bfloat16), ('row', 'col'), split_axis=0...  8.68 us
    transpose x1, local copies, waits for them, and re-layouts, on_device(): merged.reshape(clusters, total_slots, rank_dim, rank_dim)  7.41 us
    dot_general x1, matrix products, on_device(): jnp.dot(row_onehot.T, near_terms.reshape(-1, block_size * load_count), pr...  6.47 us
    dot_general x1, matrix products, on_device(): jnp.dot(col_onehot.T, near_back.reshape(-1, block_size * load_count), pre...  4.63 us
    convert_element_type x1, local copies, waits for them, and re-layouts, on_device(): couplings.reshape(-1, rank_dim, rank_dim).astype(jnp.float32)  3.76 us
    reshape x1, local copies, waits for them, and re-layouts, on_device(): merged = merged.reshape(clusters * rank_dim, total_slots * rank_dim)  3.61 us
  transfers between devices with their start and end apart: 4, of which 2 were waited for; matrix products, arithmetic and copies ran while one was open for 72% of the time, Pallas kernels for 0%

commit v1 on v0

v1 whole, which is shorter than its diff:
```python
import functools

import jax
import jax.numpy as jnp
from jax import lax
from jax.experimental import pallas as pl
from jax.experimental.pallas import tpu as pltpu
from jax.sharding import PartitionSpec as P

MESH = pl.DeviceIdType.MESH
f32 = jnp.float32
bf16 = jnp.bfloat16
UNROLL = 8
CHUNK = 16


def loop(count, body):
    if count <= 16:
        for step in range(count):
            body(step)
    else:

        def step_body(step, carry):
            body(step)
            return carry

        lax.fori_loop(0, count, step_body, 0)


def dot(a, b):
    return jnp.dot(a, b, preferred_element_type=f32)


def dot_t(a, b):
    return lax.dot_general(a, b, (((0,), (0,)), ((), ())), preferred_element_type=f32)


def sorted_index(keys_row, other_row, idx_ref, at):
    n = keys_row.shape[1]
    lane = lax.broadcasted_iota(jnp.int32, (n, n), 1)
    sub = lax.broadcasted_iota(jnp.int32, (n, n), 0)
    keys = jnp.broadcast_to(keys_row, (n, n))
    eye = lane == sub
    key_col = jnp.sum(jnp.where(eye, keys, 0), axis=1, keepdims=True)
    other_col = jnp.sum(
        jnp.where(eye, jnp.broadcast_to(other_row, (n, n)), 0), axis=1, keepdims=True
    )
    before = (keys < key_col) | ((keys == key_col) & (lane < sub))
    rank = jnp.sum(jnp.where(before, 1, 0), axis=1, keepdims=True)
    wide = (n, 128)
    lanes = lax.broadcasted_iota(jnp.int32, wide, 1)
    subs = lax.broadcasted_iota(jnp.int32, wide, 0)
    here = rank == lanes

    def pick(values):
        return jnp.sum(jnp.where(here, values, 0), axis=0, keepdims=True)

    idx_ref[at : at + 1, :] = pick(subs)
    idx_ref[at + 1 : at + 2, :] = pick(jnp.broadcast_to(key_col, wide))
    idx_ref[at + 2 : at + 3, :] = pick(jnp.broadcast_to(other_col, wide))
    upto = jnp.sum(jnp.where(key_col <= lanes, 1, 0), axis=0, keepdims=True)
    same = jnp.sum(jnp.where(key_col == lanes, 1, 0), axis=0, keepdims=True)
    idx_ref[at + 3 : at + 4, :] = jnp.where(same > 0, upto - 1, n)


def segment_products(product, idx, at, sums):
    n = sums.shape[0] - 1
    unroll = UNROLL if n % UNROLL == 0 else 1
    sums[n] = jnp.zeros(sums.shape[1:], f32)

    def body(step, total):
        terms = []
        for u in range(unroll):
            k = step * unroll + u
            terms.append(product(idx[at, k], idx[at + 2, k]))
        for u in range(unroll):
            k = step * unroll + u
            same = (idx[at + 1, k] == idx[at + 1, jnp.maximum(k - 1, 0)]) & (k > 0)
            total = total * jnp.where(same, 1.0, 0.0).astype(f32) + terms[u]
            sums[k] = total
        return total

    lax.fori_loop(0, n // unroll, body, jnp.zeros(sums.shape[1:], f32))


def kernel(
    dims,
    charges,
    loads,
    bases,
    couplings,
    near,
    near_rows,
    near_cols,
    far_rows,
    far_slots,
    send,
    potentials,
    adjoint,
    idx_v,
    idx,
    bases32,
    bases_perm,
    coeffs,
    out_f,
    in_f,
    out_r,
    in_r,
    adj32,
    merged,
    fwd32,
    sums_f,
    sums_a,
    all_loads,
    part_out,
    part_in,
    idx_sem,
    f_send,
    f_recv,
    r_send,
    r_recv,
    pair_send,
    pair_recv,
):
    cols = dims["col"]
    clusters, rank, block = bases.shape
    peers, cap = send.shape[1], send.shape[2]
    slots = peers * cap
    chunk = min(CHUNK, slots)
    chunks = slots // chunk
    group = block // rank
    tall = rank // group
    row, col, core = lax.axis_index("row"), lax.axis_index("col"), lax.axis_index("sub")
    me = row * cols + col
    other = 1 - core

    def peer_of(d):
        p = lax.rem(me + d, peers)
        return p, {"row": p // cols, "col": lax.rem(p, cols)}

    barrier = pltpu.get_barrier_semaphore()
    pl.semaphore_signal(barrier, inc=1, device_id={"sub": other}, device_id_type=MESH)

    def greet(step):
        _, device = peer_of(step + 1)
        pl.semaphore_signal(barrier, inc=1, device_id=device, device_id_type=MESH)

    loop(peers - 1, greet)

    sorted_index(near_rows[...], near_cols[...], idx_v, 0)
    sorted_index(near_cols[...], near_rows[...], idx_v, 4)
    idx_copy = pltpu.make_async_copy(idx_v, idx, idx_sem)
    idx_copy.start()

    bases32[...] = bases[...].astype(f32).reshape(clusters * rank, block)
    for c in range(clusters):
        parts = [bases32[pl.ds(c * rank + i, tall, stride=group), :] for i in range(group)]
        bases_perm[c] = jnp.concatenate(parts, axis=0).astype(bf16)
        coeffs[c] = dot(bases[c], charges[c]).astype(bf16)
        adj32[pl.ds(c, rank, stride=clusters), :] = dot(bases_perm[c], loads[c])

    pl.semaphore_wait(barrier, peers)
    pair_loads = pltpu.make_async_remote_copy(
        src_ref=loads,
        dst_ref=all_loads.at[pl.ds(core * clusters, clusters)],
        send_sem=pair_send.at[0],
        recv_sem=pair_recv.at[0],
        device_id={"sub": other},
        device_id_type=MESH,
    )
    pair_loads.start()

    def fill(p):
        for k in range(cap):
            out_f[p, k] = coeffs[jnp.maximum(send[0, p, k], 0)]

    loop(peers, fill)

    def far_copy(src, dst, send_sem, recv_sem, step):
        p, device = peer_of(step + 1)
        return pltpu.make_async_remote_copy(
            src_ref=src.at[p],
            dst_ref=dst.at[me],
            send_sem=send_sem.at[p],
            recv_sem=recv_sem.at[me],
            device_id=device,
            device_id_type=MESH,
        )

    def far_wait(src, dst, send_sem, recv_sem, step):
        p, device = peer_of(step + 1)
        return pltpu.make_async_remote_copy(
            src_ref=src.at[p],
            dst_ref=dst.at[p],
            send_sem=send_sem.at[p],
            recv_sem=recv_sem.at[p],
            device_id=device,
            device_id_type=MESH,
        )

    loop(peers - 1, lambda step: far_copy(out_f, in_f, f_send, f_recv, step).start())
    in_f[me] = out_f[me]

    key = far_slots[...] * clusters + far_rows[...]
    pairs = key.shape[1]
    adj_flat = adj32[...].astype(bf16)
    span = chunk * rank

    def merge(ch):
        cells = lax.broadcasted_iota(jnp.int32, (chunk * clusters, pairs), 0) + ch * (
            chunk * clusters
        )
        hot = jnp.where(cells == key, 1.0, 0.0).astype(bf16)
        cell = dot(hot, couplings[...])
        for t in range(chunk):
            tile = jnp.concatenate(
                [
                    cell[t * clusters : (t + 1) * clusters, a * block : (a + 1) * block]
                    for a in range(tall)
                ],
                axis=0,
            )
            turned = tile.T.astype(bf16)
            for i in range(group):
                merged[ch, t * rank : (t + 1) * rank, i * block : (i + 1) * block] = turned[
                    i * rank : (i + 1) * rank
                ]
        back = dot(merged[ch], adj_flat).astype(bf16)
        per = chunk // cap
        out_r[pl.ds(ch * per, per)] = back.reshape(per, cap, rank, block)

    loop(chunks, merge)
    loop(peers - 1, lambda step: far_copy(out_r, in_r, r_send, r_recv, step).start())
    in_r[me] = out_r[me]

    idx_copy.wait()
    segment_products(lambda b, t: dot(near[b], charges[t]), idx, 0, sums_f)
    for c in range(clusters):
        part_out[c] = sums_f[idx[3, other * clusters + c]].astype(bf16)
    pair_part = pltpu.make_async_remote_copy(
        src_ref=part_out,
        dst_ref=part_in,
        send_sem=pair_send.at[1],
        recv_sem=pair_recv.at[1],
        device_id={"sub": other},
        device_id_type=MESH,
    )
    pair_part.start()
    all_loads[pl.ds(core * clusters, clusters)] = loads[...]

    loop(peers - 1, lambda step: far_wait(out_f, in_f, f_send, f_recv, step).wait_recv())
    per = chunk // cap
    fwd32[...] = jnp.zeros(fwd32.shape, f32)

    def forward(ch):
        arrived = in_f[pl.ds(ch * per, per)].reshape(span, block)
        fwd32[...] += dot_t(merged[ch], arrived)

    loop(chunks, forward)

    pltpu.make_async_remote_copy(
        src_ref=loads,
        dst_ref=all_loads.at[pl.ds(other * clusters, clusters)],
        send_sem=pair_send.at[0],
        recv_sem=pair_recv.at[0],
        device_id={"sub": other},
        device_id_type=MESH,
    ).wait_recv()
    segment_products(lambda b, s: dot_t(near[b], all_loads[s]), idx, 4, sums_a)

    loop(peers - 1, lambda step: far_wait(out_r, in_r, r_send, r_recv, step).wait_recv())
    for c in range(clusters):
        if peers <= 16:
            total = jnp.zeros((rank, block), f32)
            for p in range(peers):
                for k in range(cap):
                    mine = jnp.where(send[0, p, k] == c, 1.0, 0.0).astype(f32)
                    total = total + in_r[p, k].astype(f32) * mine
        else:

            def gather(p, total):
                for k in range(cap):
                    mine = jnp.where(send[0, p, k] == c, 1.0, 0.0).astype(f32)
                    total = total + in_r[p, k].astype(f32) * mine
                return total

            total = lax.fori_loop(0, peers, gather, jnp.zeros((rank, block), f32))
        far = dot_t(bases[c], total.astype(bf16))
        adjoint[c] = (far + sums_a[idx[7, c]]).astype(bf16)

    pair_part.wait_recv()
    for c in range(clusters):
        far_c = fwd32[pl.ds(c, rank, stride=clusters), :].astype(bf16)
        far = dot_t(bases_perm[c], far_c)
        mine = sums_f[idx[3, core * clusters + c]]
        potentials[c] = (far + mine + part_in[c].astype(f32)).astype(bf16)

    pair_loads.wait_send()
    pair_part.wait_send()
    loop(peers - 1, lambda step: far_wait(out_f, in_f, f_send, f_recv, step).wait_send())
    loop(peers - 1, lambda step: far_wait(out_r, in_r, r_send, r_recv, step).wait_send())


def on_device(dims, *args):
    charges, _, bases, _, near, _, _, _, _, send = args
    clusters, block, width = charges.shape
    rank = bases.shape[1]
    blocks = near.shape[0]
    peers, cap = send.shape[1], send.shape[2]
    chunk = min(CHUNK, peers * cap)
    vmem = pl.BlockSpec(memory_space=pltpu.VMEM)
    smem = pl.BlockSpec(memory_space=pltpu.SMEM)
    dma = pltpu.SemaphoreType.DMA
    slot_shape = (peers, cap, rank, width)
    full = jax.ShapeDtypeStruct((clusters, block, width), bf16)
    return pl.pallas_call(
        functools.partial(kernel, dims),
        out_shape=(full, full),
        in_specs=[vmem] * 9 + [smem],
        out_specs=(vmem, vmem),
        scratch_shapes=[
            pltpu.VMEM((8, 128), jnp.int32),
            pltpu.SMEM((8, 128), jnp.int32),
            pltpu.VMEM((clusters * rank, block), f32),
            pltpu.VMEM((clusters, rank, block), bf16),
            pltpu.VMEM((clusters, rank, width), bf16),
            pltpu.VMEM(slot_shape, bf16),
            pltpu.VMEM(slot_shape, bf16),
            pltpu.VMEM(slot_shape, bf16),
            pltpu.VMEM(slot_shape, bf16),
            pltpu.VMEM((clusters * rank, width), f32),
            pltpu.VMEM((peers * cap // chunk, chunk * rank, clusters * rank), bf16),
            pltpu.VMEM((clusters * rank, width), f32),
            pltpu.VMEM((blocks + 1, block, width), f32),
            pltpu.VMEM((blocks + 1, block, width), f32),
            pltpu.VMEM((2 * clusters, block, width), bf16),
            pltpu.VMEM((clusters, block, width), bf16),
            pltpu.VMEM((clusters, block, width), bf16),
            dma,
            dma((peers,)),
            dma((peers,)),
            dma((peers,)),
            dma((peers,)),
            dma((2,)),
            dma((2,)),
        ],
        compiler_params=pltpu.CompilerParams(
            collective_id=0, has_side_effects=True, vmem_limit_bytes=52 * 1024 * 1024
        ),
        name="hierarchical",
    )(*args)


def solution(mesh):
    split = ("variant", "row", "col", "sub")
    owner = ("row", "col", "sub")
    in_specs = (
        P(split, None, None),
        P(split, None, None),
        P(split, None, None),
        P(split, None),
        P(split, None, None),
        P(owner, None),
        P(owner, None),
        P(owner, None),
        P(owner, None),
        P(owner, None, None),
    )
    out_specs = (P(split, None, None), P(split, None, None))
    return jax.shard_map(
        functools.partial(on_device, dict(mesh.shape)),
        mesh=mesh,
        in_specs=in_specs,
        out_specs=out_specs,
        check_vma=False,
    )
```

time: 138 us -> 23 us (0.17)
  other arithmetic: 34.7 us -> 0 us
  local copies, waits for them, and re-layouts: 40.8 us -> 6.95 us
  matrix products: 26.5 us -> 0 us
  Pallas kernels: 0 us -> 15.2 us
  between operations: 14.2 us -> 0.64 us
  starting transfers between devices: 11 us -> 0 us
  waiting for transfers between devices: 9.38 us -> 0 us
    scatter-add x1 -> x0, other arithmetic: 34.1 us -> none  [on_device(): merged = merged.at[pair_rows * total_slots + pair_slots].add(coupling_mats)]
    dot_general x12 -> x0, matrix products: 26.5 us -> none  [the longest x1 6.47 us: on_device(): jnp.dot(row_onehot.T, near_terms.reshape(-1, block_size * load_count), pr...]
    dot_general x6 -> x0, local copies, waits for them, and re-layouts: 16.4 us -> none  [the longest x1 3.58 us: on_device(): jnp.einsum('nij,nir->njr', near_blocks, chip_loads[block_rows], preferred...]
    pallas_call x0 -> x1, Pallas kernels: none -> 15.2 us  [on_device(): pl.pallas_call(functools.partial(kernel, dims), out_shape=(full, full), i...]
    all_to_all x2 -> x0, starting transfers between devices: 10.9 us -> none  [move_slots(): lax.all_to_all(payload.astype(jnp.bfloat16), ('row', 'col'), split_axis=0...]
    all_to_all x2 -> x0, waiting for transfers between devices: 8.68 us -> none  [move_slots(): lax.all_to_all(payload.astype(jnp.bfloat16), ('row', 'col'), split_axis=0...]
    transpose x1 -> x0, local copies, waits for them, and re-layouts: 7.41 us -> none  [on_device(): merged.reshape(clusters, total_slots, rank_dim, rank_dim)]
    unnamed x28 -> x15, local copies, waits for them, and re-layouts: 2.37 us -> 6.95 us
  transfers between devices with their start and end apart: 4 -> 0, of which waited for: 2 -> 0; matrix products, arithmetic and copies ran while one was open for 72% -> 0% of each run, Pallas kernels for 0% -> 0%
where the time goes in v1:
time: 23 us; the launch traced here: 22.8 us
  Pallas kernels  15.2 us (66%)
  local copies, waits for them, and re-layouts  6.95 us (30%)
  between operations  0.64 us (3%)
    pallas_call x1, Pallas kernels, on_device(): pl.pallas_call(functools.partial(kernel, dims), out_shape=(full, full), i...  15.2 us
    unnamed x15, local copies, waits for them, and re-layouts  6.95 us

profile of v1, /device:TPU:0, one launch (start us, length us, event | category | flops | bytes accessed | tf_op | source)
XLA Modules:
  0.0 22.8 jit_solution(18428933990434829407)
XLA Ops:
  0.6 0.8 %copy.12.send = s32[1,8,2]{2,1,0:T(8,128)S(1)} copy(s32[1,8,2]{1,2,0:T(2,128)} %param.19) | data formatting | bytes 128 | tf_op args[9]
  1.4 0.0 copy-start
  1.4 1.0 %copy-done = bf16[16,128,128]{2,1,0:T(8,128)(2,1)S(1)} copy-done((bf16[16,128,128]{2,1,0:T(8,128)(2,1)S(1)}, bf16[16,128,128]{2,1,0:T(8,128)(2,1)}, u32[]{:S(2)}) %copy-start) | copy-done | bytes 524312
  2.4 0.0 copy-start.1
  2.4 0.9 %copy-done.1 = bf16[16,32,128]{2,1,0:T(8,128)(2,1)S(1)} copy-done((bf16[16,32,128]{2,1,0:T(8,128)(2,1)S(1)}, bf16[16,32,128]{2,1,0:T(8,128)(2,1)}, u32[]{:S(2)}) %copy-start.1) | copy-done | bytes 131096
  3.3 0.0 copy-start.2
  3.3 0.7 %copy-done.2 = s32[1,256]{1,0:T(1,128)S(1)} copy-done((s32[1,256]{1,0:T(1,128)S(1)}, s32[1,256]{1,0:T(1,128)}, u32[]{:S(2)}) %copy-start.2) | copy-done | bytes 1048
  4.0 0.0 copy-start.3
  4.0 0.7 %copy-done.3 = s32[1,256]{1,0:T(1,128)S(1)} copy-done((s32[1,256]{1,0:T(1,128)S(1)}, s32[1,256]{1,0:T(1,128)}, u32[]{:S(2)}) %copy-start.3) | copy-done | bytes 1048
  4.7 0.0 copy-start.4
  4.7 0.7 %copy-done.4 = s32[1,48]{1,0:T(1,128)S(1)} copy-done((s32[1,48]{1,0:T(1,128)S(1)}, s32[1,48]{1,0:T(1,128)}, u32[]{:S(2)}) %copy-start.4) | copy-done | bytes 216
  5.3 0.0 copy-start.5
  5.3 0.7 %copy-done.5 = s32[1,48]{1,0:T(1,128)S(1)} copy-done((s32[1,48]{1,0:T(1,128)S(1)}, s32[1,48]{1,0:T(1,128)}, u32[]{:S(2)}) %copy-start.5) | copy-done | bytes 216
  6.0 15.2 %hierarchical.1 = (bf16[16,128,128]{2,1,0:T(8,128)(2,1)S(1)}, bf16[16,128,128]{2,1,0:T(8,128)(2,1)S(1)}) custom-call(bf16[16,128,128]{2,1,0:T(8,128)(2,1)S(1)} %copy-done, bf16[16,128,128]{2,1,0:T(8,128)(2,1)} %loads.1, bf16[16,32,128]{2,1,0:T(8,128)(2,1)S(1)} %copy-done.1, bf16[256,1024]{1,0:T(8,128)(2,1)} %couplings.1, bf16[48,128,128]{2,1,0:T(8,128)(2,1)} %near.1, ...), custom_call_target="tpu_custom_call" | custom-call | tf_op jit(solution)/shard_map/hierarchical/pallas_call | solution.py:316
  21.2 0.8 %copy.15 = bf16[16,128,128]{2,1,0:T(8,128)(2,1)} copy(bf16[16,128,128]{2,1,0:T(8,128)(2,1)S(1)} %get-tuple-element.4) | data formatting | bytes 1048576
  22.0 0.8 %copy.16 = bf16[16,128,128]{2,1,0:T(8,128)(2,1)} copy(bf16[16,128,128]{2,1,0:T(8,128)(2,1)S(1)} %get-tuple-element.5) | data formatting | bytes 1048576
Async XLA Ops:
  1.4 1.0 %copy-start = (bf16[16,128,128]{2,1,0:T(8,128)(2,1)S(1)}, bf16[16,128,128]{2,1,0:T(8,128)(2,1)}, u32[]{:S(2)}) copy-start(bf16[16,128,128]{2,1,0:T(8,128)(2,1)} %charges.1) | copy-start | bytes 1572868
  2.4 0.9 %copy-start.1 = (bf16[16,32,128]{2,1,0:T(8,128)(2,1)S(1)}, bf16[16,32,128]{2,1,0:T(8,128)(2,1)}, u32[]{:S(2)}) copy-start(bf16[16,32,128]{2,1,0:T(8,128)(2,1)} %bases.1) | copy-start | bytes 393220
  3.3 0.7 %copy-start.2 = (s32[1,256]{1,0:T(1,128)S(1)}, s32[1,256]{1,0:T(1,128)}, u32[]{:S(2)}) copy-start(s32[1,256]{1,0:T(1,128)} %far_rows.1) | copy-start | bytes 3076
  4.0 0.7 %copy-start.3 = (s32[1,256]{1,0:T(1,128)S(1)}, s32[1,256]{1,0:T(1,128)}, u32[]{:S(2)}) copy-start(s32[1,256]{1,0:T(1,128)} %far_slots.1) | copy-start | bytes 3076
  4.7 0.7 %copy-start.4 = (s32[1,48]{1,0:T(1,128)S(1)}, s32[1,48]{1,0:T(1,128)}, u32[]{:S(2)}) copy-start(s32[1,48]{1,0:T(1,128)} %near_rows.1) | copy-start | bytes 580
  5.3 0.7 %copy-start.5 = (s32[1,48]{1,0:T(1,128)S(1)}, s32[1,48]{1,0:T(1,128)}, u32[]{:S(2)}) copy-start(s32[1,48]{1,0:T(1,128)} %near_cols.1) | copy-start | bytes 580

commit v2 on v1

--- a/solution.py
+++ b/solution.py
@@ -85,8 +85,19 @@
 
 def kernel(
     dims,
+    charges_hbm,
+    loads_hbm,
+    bases_hbm,
+    couplings_hbm,
+    near_hbm,
+    near_rows_hbm,
+    near_cols_hbm,
+    far_rows_hbm,
+    far_slots_hbm,
+    send_hbm,
+    potentials,
+    adjoint,
     charges,
-    loads,
     bases,
     couplings,
     near,
@@ -95,8 +106,6 @@
     far_rows,
     far_slots,
     send,
-    potentials,
-    adjoint,
     idx_v,
     idx,
     bases32,
@@ -108,12 +117,14 @@
     in_r,
     adj32,
     merged,
+    place,
     fwd32,
     sums_f,
     sums_a,
     all_loads,
     part_out,
     part_in,
+    in_sem,
     idx_sem,
     f_send,
     f_recv,
@@ -124,7 +135,7 @@
 ):
     cols = dims["col"]
     clusters, rank, block = bases.shape
-    peers, cap = send.shape[1], send.shape[2]
+    cap, peers = send.shape[1], send.shape[2]
     slots = peers * cap
     chunk = min(CHUNK, slots)
     chunks = slots // chunk
@@ -138,6 +149,22 @@
         p = lax.rem(me + d, peers)
         return p, {"row": p // cols, "col": lax.rem(p, cols)}
 
+    def fetch(src, dst, at):
+        copy = pltpu.make_async_copy(src, dst, in_sem.at[at])
+        copy.start()
+        return copy
+
+    get_rows = fetch(near_rows_hbm, near_rows, 0)
+    get_cols = fetch(near_cols_hbm, near_cols, 1)
+    get_bases = fetch(bases_hbm, bases, 2)
+    get_loads = fetch(loads_hbm, all_loads.at[pl.ds(core * clusters, clusters)], 3)
+    get_charges = fetch(charges_hbm, charges, 4)
+    get_send = fetch(send_hbm, send, 5)
+    get_far_rows = fetch(far_rows_hbm, far_rows, 6)
+    get_far_slots = fetch(far_slots_hbm, far_slots, 7)
+    get_couplings = fetch(couplings_hbm, couplings, 8)
+    get_near = fetch(near_hbm, near, 9)
+
     barrier = pltpu.get_barrier_semaphore()
     pl.semaphore_signal(barrier, inc=1, device_id={"sub": other}, device_id_type=MESH)
 
@@ -147,21 +174,16 @@
 
     loop(peers - 1, greet)
 
+    get_rows.wait()
+    get_cols.wait()
     sorted_index(near_rows[...], near_cols[...], idx_v, 0)
     sorted_index(near_cols[...], near_rows[...], idx_v, 4)
     idx_copy = pltpu.make_async_copy(idx_v, idx, idx_sem)
     idx_copy.start()
 
-    bases32[...] = bases[...].astype(f32).reshape(clusters * rank, block)
-    for c in range(clusters):
-        parts = [bases32[pl.ds(c * rank + i, tall, stride=group), :] for i in range(group)]
-        bases_perm[c] = jnp.concatenate(parts, axis=0).astype(bf16)
-        coeffs[c] = dot(bases[c], charges[c]).astype(bf16)
-        adj32[pl.ds(c, rank, stride=clusters), :] = dot(bases_perm[c], loads[c])
-
     pl.semaphore_wait(barrier, peers)
     pair_loads = pltpu.make_async_remote_copy(
-        src_ref=loads,
+        src_ref=loads_hbm,
         dst_ref=all_loads.at[pl.ds(core * clusters, clusters)],
         send_sem=pair_send.at[0],
         recv_sem=pair_recv.at[0],
@@ -170,9 +192,21 @@
     )
     pair_loads.start()
 
+    get_bases.wait()
+    get_loads.wait()
+    get_charges.wait()
+    bases32[...] = bases[...].astype(f32).reshape(clusters * rank, block)
+    for c in range(clusters):
+        parts = [bases32[pl.ds(c * rank + i, tall, stride=group), :] for i in range(group)]
+        bases_perm[c] = jnp.concatenate(parts, axis=0).astype(bf16)
+        coeffs[c] = dot(bases[c], charges[c]).astype(bf16)
+        adj32[pl.ds(c, rank, stride=clusters), :] = dot(bases_perm[c], all_loads[core * clusters + c])
+
+    get_send.wait()
+
     def fill(p):
         for k in range(cap):
-            out_f[p, k] = coeffs[jnp.maximum(send[0, p, k], 0)]
+            out_f[p, k] = coeffs[jnp.maximum(send[0, k, p], 0)]
 
     loop(peers, fill)
 
@@ -201,6 +235,9 @@
     loop(peers - 1, lambda step: far_copy(out_f, in_f, f_send, f_recv, step).start())
     in_f[me] = out_f[me]
 
+    get_far_rows.wait()
+    get_far_slots.wait()
+    get_couplings.wait()
     key = far_slots[...] * clusters + far_rows[...]
     pairs = key.shape[1]
     adj_flat = adj32[...].astype(bf16)
@@ -234,6 +271,7 @@
     in_r[me] = out_r[me]
 
     idx_copy.wait()
+    get_near.wait()
     segment_products(lambda b, t: dot(near[b], charges[t]), idx, 0, sums_f)
     for c in range(clusters):
         part_out[c] = sums_f[idx[3, other * clusters + c]].astype(bf16)
@@ -246,10 +284,21 @@
         device_id_type=MESH,
     )
     pair_part.start()
-    all_loads[pl.ds(core * clusters, clusters)] = loads[...]
+
+    per = chunk // cap
+
+    def placing(ch):
+        lane = lax.broadcasted_iota(jnp.int32, (8, span), 1)
+        target = jnp.full((8, span), -1, jnp.int32)
+        for t in range(chunk):
+            own = send[0, t % cap, ch * per + t // cap]
+            target = jnp.where(lane // rank == t, own * rank + lane % rank, target)
+        rows = lax.broadcasted_iota(jnp.int32, (clusters * rank, span), 0)
+        place[ch] = jnp.where(rows == target[0:1], 1.0, 0.0).astype(bf16)
+
+    loop(chunks, placing)
 
     loop(peers - 1, lambda step: far_wait(out_f, in_f, f_send, f_recv, step).wait_recv())
-    per = chunk // cap
     fwd32[...] = jnp.zeros(fwd32.shape, f32)
 
     def forward(ch):
@@ -259,7 +308,7 @@
     loop(chunks, forward)
 
     pltpu.make_async_remote_copy(
-        src_ref=loads,
+        src_ref=loads_hbm,
         dst_ref=all_loads.at[pl.ds(other * clusters, clusters)],
         send_sem=pair_send.at[0],
         recv_sem=pair_recv.at[0],
@@ -269,22 +318,16 @@
     segment_products(lambda b, s: dot_t(near[b], all_loads[s]), idx, 4, sums_a)
 
     loop(peers - 1, lambda step: far_wait(out_r, in_r, r_send, r_recv, step).wait_recv())
+    far_adj = adj32
+    far_adj[...] = jnp.zeros(far_adj.shape, f32)
+
+    def scatter(ch):
+        returned = in_r[pl.ds(ch * per, per)].reshape(span, block)
+        far_adj[...] += dot(place[ch], returned)
+
+    loop(chunks, scatter)
     for c in range(clusters):
-        if peers <= 16:
-            total = jnp.zeros((rank, block), f32)
-            for p in range(peers):
-                for k in range(cap):
-                    mine = jnp.where(send[0, p, k] == c, 1.0, 0.0).astype(f32)
-                    total = total + in_r[p, k].astype(f32) * mine
-        else:
-
-            def gather(p, total):
-                for k in range(cap):
-                    mine = jnp.where(send[0, p, k] == c, 1.0, 0.0).astype(f32)
-                    total = total + in_r[p, k].astype(f32) * mine
-                return total
-
-            total = lax.fori_loop(0, peers, gather, jnp.zeros((rank, block), f32))
+        total = far_adj[c * rank : (c + 1) * rank]
         far = dot_t(bases[c], total.astype(bf16))
         adjoint[c] = (far + sums_a[idx[7, c]]).astype(bf16)
 
@@ -302,23 +345,32 @@
 
 
 def on_device(dims, *args):
-    charges, _, bases, _, near, _, _, _, _, send = args
+    args = args[:-1] + (jnp.transpose(args[-1], (0, 2, 1)),)
+    charges, loads, bases, couplings, near, near_rows, near_cols, far_rows, far_slots, send = args
     clusters, block, width = charges.shape
     rank = bases.shape[1]
     blocks = near.shape[0]
-    peers, cap = send.shape[1], send.shape[2]
+    cap, peers = send.shape[1], send.shape[2]
     chunk = min(CHUNK, peers * cap)
     vmem = pl.BlockSpec(memory_space=pltpu.VMEM)
-    smem = pl.BlockSpec(memory_space=pltpu.SMEM)
     dma = pltpu.SemaphoreType.DMA
     slot_shape = (peers, cap, rank, width)
     full = jax.ShapeDtypeStruct((clusters, block, width), bf16)
     return pl.pallas_call(
         functools.partial(kernel, dims),
         out_shape=(full, full),
-        in_specs=[vmem] * 9 + [smem],
+        in_specs=[pl.BlockSpec(memory_space=pl.ANY)] * 10,
         out_specs=(vmem, vmem),
         scratch_shapes=[
+            pltpu.VMEM(charges.shape, bf16),
+            pltpu.VMEM(bases.shape, bf16),
+            pltpu.VMEM(couplings.shape, bf16),
+            pltpu.VMEM(near.shape, bf16),
+            pltpu.VMEM(near_rows.shape, jnp.int32),
+            pltpu.VMEM(near_cols.shape, jnp.int32),
+            pltpu.VMEM(far_rows.shape, jnp.int32),
+            pltpu.VMEM(far_slots.shape, jnp.int32),
+            pltpu.SMEM(send.shape, jnp.int32),
             pltpu.VMEM((8, 128), jnp.int32),
             pltpu.SMEM((8, 128), jnp.int32),
             pltpu.VMEM((clusters * rank, block), f32),
@@ -330,12 +382,14 @@
             pltpu.VMEM(slot_shape, bf16),
             pltpu.VMEM((clusters * rank, width), f32),
             pltpu.VMEM((peers * cap // chunk, chunk * rank, clusters * rank), bf16),
+            pltpu.VMEM((peers * cap // chunk, clusters * rank, chunk * rank), bf16),
             pltpu.VMEM((clusters * rank, width), f32),
             pltpu.VMEM((blocks + 1, block, width), f32),
             pltpu.VMEM((blocks + 1, block, width), f32),
             pltpu.VMEM((2 * clusters, block, width), bf16),
             pltpu.VMEM((clusters, block, width), bf16),
             pltpu.VMEM((clusters, block, width), bf16),
+            dma((10,)),
             dma,
             dma((peers,)),
             dma((peers,)),
@@ -345,7 +399,7 @@
             dma((2,)),
         ],
         compiler_params=pltpu.CompilerParams(
-            collective_id=0, has_side_effects=True, vmem_limit_bytes=52 * 1024 * 1024
+            collective_id=0, has_side_effects=True, vmem_limit_bytes=62 * 1024 * 1024
         ),
         name="hierarchical",
     )(*args)

time: 23 us -> 19.8 us (0.86)
  local copies, waits for them, and re-layouts: 6.95 us -> 3.77 us
    unnamed x15 -> x2, local copies, waits for them, and re-layouts: 6.95 us -> 3.77 us
where the time goes in v2:
time: 19.8 us; the launch traced here: 19.6 us
  Pallas kernels  15.2 us (77%)
  local copies, waits for them, and re-layouts  3.77 us (19%)
  between operations  0.64 us (3%)
    pallas_call x1, Pallas kernels, on_device(): pl.pallas_call(functools.partial(kernel, dims), out_shape=(full, full), i...  15.2 us
    unnamed x2, local copies, waits for them, and re-layouts  3.77 us

profile of v2, /device:TPU:0, one launch (start us, length us, event | category | flops | bytes accessed | tf_op | source)
XLA Modules:
  0.0 19.6 jit_solution(893888216559433991)
XLA Ops:
  0.6 15.2 %hierarchical.1 = (bf16[16,128,128]{2,1,0:T(8,128)(2,1)}, bf16[16,128,128]{2,1,0:T(8,128)(2,1)}) custom-call(bf16[16,128,128]{2,1,0:T(8,128)(2,1)} %charges_hbm.1, bf16[16,128,128]{2,1,0:T(8,128)(2,1)} %loads_hbm.1, bf16[16,32,128]{2,1,0:T(8,128)(2,1)} %bases_hbm.1, bf16[256,1024]{1,0:T(8,128)(2,1)} %couplings_hbm.1, bf16[48,128,128]{2,1,0:T(8,128)(2,1)} %near_hbm.1, ...), custom_call_target="tpu_custom_call" | custom-call | tf_op jit(solution)/shard_map/hierarchical/pallas_call | solution.py:359
  15.8 1.9 %copy.14 = bf16[16,128,128]{2,1,0:T(8,128)(2,1)} copy(bf16[16,128,128]{2,1,0:T(8,128)(2,1)} %get-tuple-element.4) | data formatting | bytes 1048576
  17.7 1.9 %copy.15 = bf16[16,128,128]{2,1,0:T(8,128)(2,1)} copy(bf16[16,128,128]{2,1,0:T(8,128)(2,1)} %get-tuple-element.5) | data formatting | bytes 1048576

commit v3 on v2

--- a/solution.py
+++ b/solution.py
@@ -146,7 +146,13 @@
     other = 1 - core
 
     def peer_of(d):
-        p = lax.rem(me + d, peers)
+        if peers & (peers - 1):
+            p = lax.rem(me + d, peers)
+        else:
+            p, bit = 0, 1
+            while bit < peers:
+                p = p + lax.rem(me // bit + (peers - d) // bit, 2) * bit
+                bit *= 2
         return p, {"row": p // cols, "col": lax.rem(p, cols)}
 
     def fetch(src, dst, at):
@@ -154,15 +160,15 @@
         copy.start()
         return copy
 
-    get_rows = fetch(near_rows_hbm, near_rows, 0)
-    get_cols = fetch(near_cols_hbm, near_cols, 1)
-    get_bases = fetch(bases_hbm, bases, 2)
+    get_bases = fetch(bases_hbm, bases, 0)
+    get_charges = fetch(charges_hbm, charges, 1)
+    get_send = fetch(send_hbm, send, 2)
     get_loads = fetch(loads_hbm, all_loads.at[pl.ds(core * clusters, clusters)], 3)
-    get_charges = fetch(charges_hbm, charges, 4)
-    get_send = fetch(send_hbm, send, 5)
-    get_far_rows = fetch(far_rows_hbm, far_rows, 6)
-    get_far_slots = fetch(far_slots_hbm, far_slots, 7)
-    get_couplings = fetch(couplings_hbm, couplings, 8)
+    get_couplings = fetch(couplings_hbm, couplings, 4)
+    get_far_rows = fetch(far_rows_hbm, far_rows, 5)
+    get_far_slots = fetch(far_slots_hbm, far_slots, 6)
+    get_rows = fetch(near_rows_hbm, near_rows, 7)
+    get_cols = fetch(near_cols_hbm, near_cols, 8)
     get_near = fetch(near_hbm, near, 9)
 
     barrier = pltpu.get_barrier_semaphore()
@@ -174,34 +180,10 @@
 
     loop(peers - 1, greet)
 
-    get_rows.wait()
-    get_cols.wait()
-    sorted_index(near_rows[...], near_cols[...], idx_v, 0)
-    sorted_index(near_cols[...], near_rows[...], idx_v, 4)
-    idx_copy = pltpu.make_async_copy(idx_v, idx, idx_sem)
-    idx_copy.start()
-
-    pl.semaphore_wait(barrier, peers)
-    pair_loads = pltpu.make_async_remote_copy(
-        src_ref=loads_hbm,
-        dst_ref=all_loads.at[pl.ds(core * clusters, clusters)],
-        send_sem=pair_send.at[0],
-        recv_sem=pair_recv.at[0],
-        device_id={"sub": other},
-        device_id_type=MESH,
-    )
-    pair_loads.start()
-
     get_bases.wait()
-    get_loads.wait()
     get_charges.wait()
-    bases32[...] = bases[...].astype(f32).reshape(clusters * rank, block)
     for c in range(clusters):
-        parts = [bases32[pl.ds(c * rank + i, tall, stride=group), :] for i in range(group)]
-        bases_perm[c] = jnp.concatenate(parts, axis=0).astype(bf16)
         coeffs[c] = dot(bases[c], charges[c]).astype(bf16)
-        adj32[pl.ds(c, rank, stride=clusters), :] = dot(bases_perm[c], all_loads[core * clusters + c])
-
     get_send.wait()
 
     def fill(p):
@@ -209,6 +191,7 @@
             out_f[p, k] = coeffs[jnp.maximum(send[0, k, p], 0)]
 
     loop(peers, fill)
+    pl.semaphore_wait(barrier, peers)
 
     def far_copy(src, dst, send_sem, recv_sem, step):
         p, device = peer_of(step + 1)
@@ -234,6 +217,24 @@
 
     loop(peers - 1, lambda step: far_copy(out_f, in_f, f_send, f_recv, step).start())
     in_f[me] = out_f[me]
+    pair_loads = pltpu.make_async_remote_copy(
+        src_ref=loads_hbm,
+        dst_ref=all_loads.at[pl.ds(core * clusters, clusters)],
+        send_sem=pair_send.at[0],
+        recv_sem=pair_recv.at[0],
+        device_id={"sub": other},
+        device_id_type=MESH,
+    )
+    pair_loads.start()
+
+    get_loads.wait()
+    bases32[...] = bases[...].astype(f32).reshape(clusters * rank, block)
+    for c in range(clusters):
+        parts = [bases32[pl.ds(c * rank + i, tall, stride=group), :] for i in range(group)]
+        bases_perm[c] = jnp.concatenate(parts, axis=0).astype(bf16)
+        adj32[pl.ds(c, rank, stride=clusters), :] = dot(
+            bases_perm[c], all_loads[core * clusters + c]
+        )
 
     get_far_rows.wait()
     get_far_slots.wait()
@@ -270,6 +271,13 @@
     loop(peers - 1, lambda step: far_copy(out_r, in_r, r_send, r_recv, step).start())
     in_r[me] = out_r[me]
 
+    get_rows.wait()
+    get_cols.wait()
+    sorted_index(near_rows[...], near_cols[...], idx_v, 0)
+    sorted_index(near_cols[...], near_rows[...], idx_v, 4)
+    idx_copy = pltpu.make_async_copy(idx_v, idx, idx_sem)
+    idx_copy.start()
+
     idx_copy.wait()
     get_near.wait()
     segment_products(lambda b, t: dot(near[b], charges[t]), idx, 0, sums_f)
@@ -344,6 +352,15 @@
     loop(peers - 1, lambda step: far_wait(out_r, in_r, r_send, r_recv, step).wait_send())
 
 
+def write_out(potentials, adjoint, potentials_hbm, adjoint_hbm, sem):
+    first = pltpu.make_async_copy(potentials, potentials_hbm, sem.at[0])
+    second = pltpu.make_async_copy(adjoint, adjoint_hbm, sem.at[1])
+    first.start()
+    second.start()
+    first.wait()
+    second.wait()
+
+
 def on_device(dims, *args):
     args = args[:-1] + (jnp.transpose(args[-1], (0, 2, 1)),)
     charges, loads, bases, couplings, near, near_rows, near_cols, far_rows, far_slots, send = args
@@ -356,10 +373,10 @@
     dma = pltpu.SemaphoreType.DMA
     slot_shape = (peers, cap, rank, width)
     full = jax.ShapeDtypeStruct((clusters, block, width), bf16)
-    return pl.pallas_call(
+    results = pl.pallas_call(
         functools.partial(kernel, dims),
-        out_shape=(full, full),
-        in_specs=[pl.BlockSpec(memory_space=pl.ANY)] * 10,
+        out_shape=(pltpu.VMEM(full.shape, bf16),) * 2,
+        in_specs=[pl.BlockSpec(memory_space=pltpu.HBM)] * 10,
         out_specs=(vmem, vmem),
         scratch_shapes=[
             pltpu.VMEM(charges.shape, bf16),
@@ -399,10 +416,18 @@
             dma((2,)),
         ],
         compiler_params=pltpu.CompilerParams(
-            collective_id=0, has_side_effects=True, vmem_limit_bytes=62 * 1024 * 1024
+            collective_id=0, has_side_effects=True, vmem_limit_bytes=54 * 1024 * 1024
         ),
         name="hierarchical",
     )(*args)
+    return pl.pallas_call(
+        write_out,
+        out_shape=(full, full),
+        in_specs=[vmem] * 2,
+        out_specs=(pl.BlockSpec(memory_space=pltpu.HBM),) * 2,
+        scratch_shapes=[dma((2,))],
+        name="write_out",
+    )(*results)
 
 
 def solution(mesh):

time: 19.8 us -> 19.8 us (level)
  Pallas kernels: 15.2 us -> 17.4 us
  local copies, waits for them, and re-layouts: 3.77 us -> 1.58 us
    pallas_call x1 -> x2, Pallas kernels: 15.2 us -> 17.4 us  [the longest x1 15.3 us: on_device(): pl.pallas_call(functools.partial(kernel, dims), out_shape=(pltpu.VMEM(ful...]
    unnamed x2 -> x4, local copies, waits for them, and re-layouts: 3.77 us -> 1.58 us
where the time goes in v3:
time: 19.8 us; the launch traced here: 19.7 us
  Pallas kernels  17.4 us (88%)
  local copies, waits for them, and re-layouts  1.58 us (8%)
  between operations  0.65 us (3%)
    pallas_call x1, Pallas kernels, on_device(): pl.pallas_call(functools.partial(kernel, dims), out_shape=(pltpu.VMEM(ful...  15.3 us
    pallas_call x1, Pallas kernels, on_device(): pl.pallas_call(write_out, out_shape=(full, full), in_specs=[vmem] * 2, ou...  2.18 us
    unnamed x4, local copies, waits for them, and re-layouts  1.58 us

profile of v3, /device:TPU:0, one launch (start us, length us, event | category | flops | bytes accessed | tf_op | source)
XLA Modules:
  0.0 19.7 jit_solution(10712335037799326124)
XLA Ops:
  0.6 15.3 %hierarchical.1 = (bf16[16,128,128]{2,1,0:T(8,128)(2,1)S(1)}, bf16[16,128,128]{2,1,0:T(8,128)(2,1)S(1)}) custom-call(bf16[16,128,128]{2,1,0:T(8,128)(2,1)} %charges_hbm.1, bf16[16,128,128]{2,1,0:T(8,128)(2,1)} %loads_hbm.1, bf16[16,32,128]{2,1,0:T(8,128)(2,1)} %bases_hbm.1, bf16[256,1024]{1,0:T(8,128)(2,1)} %couplings_hbm.1, bf16[48,128,128]{2,1,0:T(8,128)(2,1)} %near_hbm.1, ...), custom_call_target="tpu_custom_call" | custom-call | tf_op jit(solution)/shard_map/hierarchical/pallas_call | solution.py:376
  15.9 0.0 copy-start
  15.9 0.8 %copy-done = bf16[16,128,128]{2,1,0:T(8,128)(2,1)} copy-done((bf16[16,128,128]{2,1,0:T(8,128)(2,1)}, bf16[16,128,128]{2,1,0:T(8,128)(2,1)S(1)}, u32[]{:S(2)}) %copy-start) | copy-done | bytes 524312
  16.7 0.0 copy-start.1
  16.7 0.8 %copy-done.1 = bf16[16,128,128]{2,1,0:T(8,128)(2,1)} copy-done((bf16[16,128,128]{2,1,0:T(8,128)(2,1)}, bf16[16,128,128]{2,1,0:T(8,128)(2,1)S(1)}, u32[]{:S(2)}) %copy-start.1) | copy-done | bytes 524312
  17.5 2.2 %write_out.1 = (bf16[16,128,128]{2,1,0:T(8,128)(2,1)}, bf16[16,128,128]{2,1,0:T(8,128)(2,1)}) custom-call(bf16[16,128,128]{2,1,0:T(8,128)(2,1)} %copy-done, bf16[16,128,128]{2,1,0:T(8,128)(2,1)} %copy-done.1), custom_call_target="tpu_custom_call" | custom-call | tf_op jit(solution)/shard_map/write_out/pallas_call | solution.py:423
Async XLA Ops:
  15.9 0.8 %copy-start = (bf16[16,128,128]{2,1,0:T(8,128)(2,1)}, bf16[16,128,128]{2,1,0:T(8,128)(2,1)S(1)}, u32[]{:S(2)}) copy-start(bf16[16,128,128]{2,1,0:T(8,128)(2,1)S(1)} %get-tuple-element.4.potentials) | copy-start | bytes 1572868
  16.7 0.8 %copy-start.1 = (bf16[16,128,128]{2,1,0:T(8,128)(2,1)}, bf16[16,128,128]{2,1,0:T(8,128)(2,1)S(1)}, u32[]{:S(2)}) copy-start(bf16[16,128,128]{2,1,0:T(8,128)(2,1)S(1)} %get-tuple-element.5.adjoint) | copy-start | bytes 1572868

commit v4 on v3

--- a/solution.py
+++ b/solution.py
@@ -12,6 +12,7 @@
 bf16 = jnp.bfloat16
 UNROLL = 8
 CHUNK = 16
+PIECES = 4
 
 
 def loop(count, body):
@@ -96,9 +97,10 @@
     far_slots_hbm,
     send_hbm,
     potentials,
-    adjoint,
+    near_adj,
+    far_adj,
+    bases,
     charges,
-    bases,
     couplings,
     near,
     near_rows,
@@ -160,8 +162,15 @@
         copy.start()
         return copy
 
+    def fetch_pieces(src, dst, at):
+        size = src.shape[0] // PIECES
+        return [
+            fetch(src.at[pl.ds(i * size, size)], dst.at[pl.ds(i * size, size)], at + i)
+            for i in range(PIECES)
+        ]
+
     get_bases = fetch(bases_hbm, bases, 0)
-    get_charges = fetch(charges_hbm, charges, 1)
+    get_charges = fetch_pieces(charges_hbm, charges, 10)
     get_send = fetch(send_hbm, send, 2)
     get_loads = fetch(loads_hbm, all_loads.at[pl.ds(core * clusters, clusters)], 3)
     get_couplings = fetch(couplings_hbm, couplings, 4)
@@ -169,7 +178,7 @@
     get_far_slots = fetch(far_slots_hbm, far_slots, 6)
     get_rows = fetch(near_rows_hbm, near_rows, 7)
     get_cols = fetch(near_cols_hbm, near_cols, 8)
-    get_near = fetch(near_hbm, near, 9)
+    get_near = fetch_pieces(near_hbm, near, 10 + PIECES)
 
     barrier = pltpu.get_barrier_semaphore()
     pl.semaphore_signal(barrier, inc=1, device_id={"sub": other}, device_id_type=MESH)
@@ -181,8 +190,9 @@
     loop(peers - 1, greet)
 
     get_bases.wait()
-    get_charges.wait()
     for c in range(clusters):
+        if c % (clusters // PIECES) == 0:
+            get_charges[c // (clusters // PIECES)].wait()
         coeffs[c] = dot(bases[c], charges[c]).astype(bf16)
     get_send.wait()
 
@@ -279,7 +289,8 @@
     idx_copy.start()
 
     idx_copy.wait()
-    get_near.wait()
+    for piece in get_near:
+        piece.wait()
     segment_products(lambda b, t: dot(near[b], charges[t]), idx, 0, sums_f)
     for c in range(clusters):
         part_out[c] = sums_f[idx[3, other * clusters + c]].astype(bf16)
@@ -325,20 +336,8 @@
     ).wait_recv()
     segment_products(lambda b, s: dot_t(near[b], all_loads[s]), idx, 4, sums_a)
 
-    loop(peers - 1, lambda step: far_wait(out_r, in_r, r_send, r_recv, step).wait_recv())
-    far_adj = adj32
-    far_adj[...] = jnp.zeros(far_adj.shape, f32)
-
-    def scatter(ch):
-        returned = in_r[pl.ds(ch * per, per)].reshape(span, block)
-        far_adj[...] += dot(place[ch], returned)
-
-    loop(chunks, scatter)
     for c in range(clusters):
-        total = far_adj[c * rank : (c + 1) * rank]
-        far = dot_t(bases[c], total.astype(bf16))
-        adjoint[c] = (far + sums_a[idx[7, c]]).astype(bf16)
-
+        near_adj[c] = sums_a[idx[7, c]]
     pair_part.wait_recv()
     for c in range(clusters):
         far_c = fwd32[pl.ds(c, rank, stride=clusters), :].astype(bf16)
@@ -346,19 +345,45 @@
         mine = sums_f[idx[3, core * clusters + c]]
         potentials[c] = (far + mine + part_in[c].astype(f32)).astype(bf16)
 
+    loop(peers - 1, lambda step: far_wait(out_r, in_r, r_send, r_recv, step).wait_recv())
+    total = jnp.zeros(adj32.shape, f32)
+    if chunks == 1:
+        total = dot(place[0], in_r[...].reshape(span, block))
+    else:
+        adj32[...] = total
+
+        def scatter(ch):
+            returned = in_r[pl.ds(ch * per, per)].reshape(span, block)
+            adj32[...] += dot(place[ch], returned)
+
+        loop(chunks, scatter)
+        total = adj32[...]
+    far_adj[...] = total.astype(bf16).reshape(clusters, rank, block)
+
     pair_loads.wait_send()
     pair_part.wait_send()
     loop(peers - 1, lambda step: far_wait(out_f, in_f, f_send, f_recv, step).wait_send())
     loop(peers - 1, lambda step: far_wait(out_r, in_r, r_send, r_recv, step).wait_send())
 
 
-def write_out(potentials, adjoint, potentials_hbm, adjoint_hbm, sem):
-    first = pltpu.make_async_copy(potentials, potentials_hbm, sem.at[0])
-    second = pltpu.make_async_copy(adjoint, adjoint_hbm, sem.at[1])
-    first.start()
-    second.start()
-    first.wait()
-    second.wait()
+def finish(potentials, near_adj, far_adj, bases, potentials_hbm, adjoint_hbm, adjoint, sem):
+    clusters = potentials.shape[0]
+    size = clusters // PIECES
+    copies = []
+
+    def write(src, dst, piece, at):
+        part = pl.ds(piece * size, size)
+        copies.append(pltpu.make_async_copy(src.at[part], dst.at[part], sem.at[at]))
+        copies[-1].start()
+
+    for piece in range(PIECES):
+        write(potentials, potentials_hbm, piece, piece)
+    for piece in range(PIECES):
+        for c in range(piece * size, (piece + 1) * size):
+            adjoint[c] = (dot_t(bases[c], far_adj[c]) + near_adj[c]).astype(bf16)
+        write(adjoint, adjoint_hbm, piece, PIECES + piece)
+    for copy in copies:
+        copy.wait()
 
 
 def on_device(dims, *args):
@@ -375,12 +400,16 @@
     full = jax.ShapeDtypeStruct((clusters, block, width), bf16)
     results = pl.pallas_call(
         functools.partial(kernel, dims),
-        out_shape=(pltpu.VMEM(full.shape, bf16),) * 2,
+        out_shape=(
+            pltpu.VMEM(full.shape, bf16),
+            pltpu.VMEM(full.shape, f32),
+            pltpu.VMEM((clusters, rank, width), bf16),
+            pltpu.VMEM(bases.shape, bf16),
+        ),
         in_specs=[pl.BlockSpec(memory_space=pltpu.HBM)] * 10,
-        out_specs=(vmem, vmem),
+        out_specs=(vmem,) * 4,
         scratch_shapes=[
             pltpu.VMEM(charges.shape, bf16),
-            pltpu.VMEM(bases.shape, bf16),
             pltpu.VMEM(couplings.shape, bf16),
             pltpu.VMEM(near.shape, bf16),
             pltpu.VMEM(near_rows.shape, jnp.int32),
@@ -406,7 +435,7 @@
             pltpu.VMEM((2 * clusters, block, width), bf16),
             pltpu.VMEM((clusters, block, width), bf16),
             pltpu.VMEM((clusters, block, width), bf16),
-            dma((10,)),
+            dma((10 + 2 * PIECES,)),
             dma,
             dma((peers,)),
             dma((peers,)),
@@ -421,12 +450,13 @@
         name="hierarchical",
     )(*args)
     return pl.pallas_call(
-        write_out,
+        finish,
         out_shape=(full, full),
-        in_specs=[vmem] * 2,
+        in_specs=[vmem] * 4,
         out_specs=(pl.BlockSpec(memory_space=pltpu.HBM),) * 2,
-        scratch_shapes=[dma((2,))],
-        name="write_out",
+        scratch_shapes=[pltpu.VMEM(full.shape, bf16), dma((2 * PIECES,))],
+        compiler_params=pltpu.CompilerParams(vmem_limit_bytes=4 * 1024 * 1024),
+        name="finish",
     )(*results)
 
 

time: 19.8 us -> 16.9 us (0.85)
  local copies, waits for them, and re-layouts: 1.58 us -> 0 us
  Pallas kernels: 17.4 us -> 16.1 us
    unnamed x4 -> x0, local copies, waits for them, and re-layouts: 1.58 us -> none
    pallas_call x1, Pallas kernels: 2.18 us -> 1.1 us  [on_device(): pl.pallas_call(finish, out_shape=(full, full), in_specs=[vmem] * 4, out_s...]
    pallas_call x1, Pallas kernels: 15.3 us -> 15 us  [on_device(): pl.pallas_call(functools.partial(kernel, dims), out_shape=(pltpu.VMEM(ful...]
where the time goes in v4:
time: 16.9 us; the launch traced here: 16.7 us
  Pallas kernels  16.1 us (95%)
  between operations  0.64 us (4%)
    pallas_call x1, Pallas kernels, on_device(): pl.pallas_call(functools.partial(kernel, dims), out_shape=(pltpu.VMEM(ful...  15 us
    pallas_call x1, Pallas kernels, on_device(): pl.pallas_call(finish, out_shape=(full, full), in_specs=[vmem] * 4, out_s...  1.1 us

profile of v4, /device:TPU:0, one launch (start us, length us, event | category | flops | bytes accessed | tf_op | source)
XLA Modules:
  0.0 16.7 jit_solution(16658183931632175192)
XLA Ops:
  0.6 15.0 %hierarchical.1 = (bf16[16,128,128]{2,1,0:T(8,128)(2,1)S(1)}, f32[16,128,128]{2,1,0:T(8,128)S(1)}, bf16[16,32,128]{2,1,0:T(8,128)(2,1)S(1)}, bf16[16,32,128]{2,1,0:T(8,128)(2,1)S(1)}) custom-call(bf16[16,128,128]{2,1,0:T(8,128)(2,1)} %charges_hbm.1, bf16[16,128,128]{2,1,0:T(8,128)(2,1)} %loads_hbm.1, bf16[16,32,128]{2,1,0:T(8,128)(2,1)} %bases_hbm.1, ...), custom_call_target="tpu_custom_call" | custom-call | tf_op jit(solution)/shard_map/hierarchical/pallas_call | solution.py:401
  15.6 1.1 %finish.1 = (bf16[16,128,128]{2,1,0:T(8,128)(2,1)}, bf16[16,128,128]{2,1,0:T(8,128)(2,1)}) custom-call(bf16[16,128,128]{2,1,0:T(8,128)(2,1)S(1)} %get-tuple-element.6.potentials, f32[16,128,128]{2,1,0:T(8,128)S(1)} %get-tuple-element.7.near_adj, bf16[16,32,128]{2,1,0:T(8,128)(2,1)S(1)} %get-tuple-element.8.far_adj, ...), custom_call_target="tpu_custom_call" | custom-call | tf_op jit(solution)/shard_map/finish/pallas_call | solution.py:452

commit v5 on v4

--- a/solution.py
+++ b/solution.py
@@ -157,6 +157,15 @@
                 bit *= 2
         return p, {"row": p // cols, "col": lax.rem(p, cols)}
 
+    barrier = pltpu.get_barrier_semaphore()
+    pl.semaphore_signal(barrier, inc=1, device_id={"sub": other}, device_id_type=MESH)
+
+    def greet(step):
+        _, device = peer_of(step + 1)
+        pl.semaphore_signal(barrier, inc=1, device_id=device, device_id_type=MESH)
+
+    loop(peers - 1, greet)
+
     def fetch(src, dst, at):
         copy = pltpu.make_async_copy(src, dst, in_sem.at[at])
         copy.start()
@@ -179,15 +188,6 @@
     get_rows = fetch(near_rows_hbm, near_rows, 7)
     get_cols = fetch(near_cols_hbm, near_cols, 8)
     get_near = fetch_pieces(near_hbm, near, 10 + PIECES)
-
-    barrier = pltpu.get_barrier_semaphore()
-    pl.semaphore_signal(barrier, inc=1, device_id={"sub": other}, device_id_type=MESH)
-
-    def greet(step):
-        _, device = peer_of(step + 1)
-        pl.semaphore_signal(barrier, inc=1, device_id=device, device_id_type=MESH)
-
-    loop(peers - 1, greet)
 
     get_bases.wait()
     for c in range(clusters):
@@ -317,15 +317,6 @@
 
     loop(chunks, placing)
 
-    loop(peers - 1, lambda step: far_wait(out_f, in_f, f_send, f_recv, step).wait_recv())
-    fwd32[...] = jnp.zeros(fwd32.shape, f32)
-
-    def forward(ch):
-        arrived = in_f[pl.ds(ch * per, per)].reshape(span, block)
-        fwd32[...] += dot_t(merged[ch], arrived)
-
-    loop(chunks, forward)
-
     pltpu.make_async_remote_copy(
         src_ref=loads_hbm,
         dst_ref=all_loads.at[pl.ds(other * clusters, clusters)],
@@ -335,6 +326,15 @@
         device_id_type=MESH,
     ).wait_recv()
     segment_products(lambda b, s: dot_t(near[b], all_loads[s]), idx, 4, sums_a)
+
+    loop(peers - 1, lambda step: far_wait(out_f, in_f, f_send, f_recv, step).wait_recv())
+    fwd32[...] = jnp.zeros(fwd32.shape, f32)
+
+    def forward(ch):
+        arrived = in_f[pl.ds(ch * per, per)].reshape(span, block)
+        fwd32[...] += dot_t(arrived, merged[ch]).T
+
+    loop(chunks, forward)
 
     for c in range(clusters):
         near_adj[c] = sums_a[idx[7, c]]

time: 16.9 us -> 15.8 us (0.935)
  Pallas kernels: 16.1 us -> 15 us
    pallas_call x1, Pallas kernels: 15 us -> 13.9 us  [on_device(): pl.pallas_call(functools.partial(kernel, dims), out_shape=(pltpu.VMEM(ful...]
where the time goes in v5:
time: 15.8 us; the launch traced here: 15.6 us
  Pallas kernels  15 us (95%)
  between operations  0.64 us (4%)
    pallas_call x1, Pallas kernels, on_device(): pl.pallas_call(functools.partial(kernel, dims), out_shape=(pltpu.VMEM(ful...  13.9 us
    pallas_call x1, Pallas kernels, on_device(): pl.pallas_call(finish, out_shape=(full, full), in_specs=[vmem] * 4, out_s...  1.1 us

profile of v5, /device:TPU:0, one launch (start us, length us, event | category | flops | bytes accessed | tf_op | source)
XLA Modules:
  0.0 15.6 jit_solution(16576077302044907000)
XLA Ops:
  0.6 13.9 %hierarchical.1 = (bf16[16,128,128]{2,1,0:T(8,128)(2,1)S(1)}, f32[16,128,128]{2,1,0:T(8,128)S(1)}, bf16[16,32,128]{2,1,0:T(8,128)(2,1)S(1)}, bf16[16,32,128]{2,1,0:T(8,128)(2,1)S(1)}) custom-call(bf16[16,128,128]{2,1,0:T(8,128)(2,1)} %charges_hbm.1, bf16[16,128,128]{2,1,0:T(8,128)(2,1)} %loads_hbm.1, bf16[16,32,128]{2,1,0:T(8,128)(2,1)} %bases_hbm.1, ...), custom_call_target="tpu_custom_call" | custom-call | tf_op jit(solution)/shard_map/hierarchical/pallas_call | solution.py:401
  14.5 1.1 %finish.1 = (bf16[16,128,128]{2,1,0:T(8,128)(2,1)}, bf16[16,128,128]{2,1,0:T(8,128)(2,1)}) custom-call(bf16[16,128,128]{2,1,0:T(8,128)(2,1)S(1)} %get-tuple-element.6.potentials, f32[16,128,128]{2,1,0:T(8,128)S(1)} %get-tuple-element.7.near_adj, bf16[16,32,128]{2,1,0:T(8,128)(2,1)S(1)} %get-tuple-element.8.far_adj, ...), custom_call_target="tpu_custom_call" | custom-call | tf_op jit(solution)/shard_map/finish/pallas_call | solution.py:452

commit v6 on v5

--- a/solution.py
+++ b/solution.py
@@ -12,7 +12,7 @@
 bf16 = jnp.bfloat16
 UNROLL = 8
 CHUNK = 16
-PIECES = 4
+PIECES = 2
 
 
 def loop(count, body):
@@ -157,15 +157,6 @@
                 bit *= 2
         return p, {"row": p // cols, "col": lax.rem(p, cols)}
 
-    barrier = pltpu.get_barrier_semaphore()
-    pl.semaphore_signal(barrier, inc=1, device_id={"sub": other}, device_id_type=MESH)
-
-    def greet(step):
-        _, device = peer_of(step + 1)
-        pl.semaphore_signal(barrier, inc=1, device_id=device, device_id_type=MESH)
-
-    loop(peers - 1, greet)
-
     def fetch(src, dst, at):
         copy = pltpu.make_async_copy(src, dst, in_sem.at[at])
         copy.start()
@@ -180,15 +171,17 @@
 
     get_bases = fetch(bases_hbm, bases, 0)
     get_charges = fetch_pieces(charges_hbm, charges, 10)
+    barrier = pltpu.get_barrier_semaphore()
+    pl.semaphore_signal(barrier, inc=1, device_id={"sub": other}, device_id_type=MESH)
+
+    def greet(step):
+        _, device = peer_of(step + 1)
+        pl.semaphore_signal(barrier, inc=1, device_id=device, device_id_type=MESH)
+
+    loop(peers - 1, greet)
+
     get_send = fetch(send_hbm, send, 2)
     get_loads = fetch(loads_hbm, all_loads.at[pl.ds(core * clusters, clusters)], 3)
-    get_couplings = fetch(couplings_hbm, couplings, 4)
-    get_far_rows = fetch(far_rows_hbm, far_rows, 5)
-    get_far_slots = fetch(far_slots_hbm, far_slots, 6)
-    get_rows = fetch(near_rows_hbm, near_rows, 7)
-    get_cols = fetch(near_cols_hbm, near_cols, 8)
-    get_near = fetch_pieces(near_hbm, near, 10 + PIECES)
-
     get_bases.wait()
     for c in range(clusters):
         if c % (clusters // PIECES) == 0:
@@ -226,6 +219,13 @@
         )
 
     loop(peers - 1, lambda step: far_copy(out_f, in_f, f_send, f_recv, step).start())
+    get_couplings = fetch(couplings_hbm, couplings, 4)
+    get_far_rows = fetch(far_rows_hbm, far_rows, 5)
+    get_far_slots = fetch(far_slots_hbm, far_slots, 6)
+    get_rows = fetch(near_rows_hbm, near_rows, 7)
+    get_cols = fetch(near_cols_hbm, near_cols, 8)
+    get_near = fetch_pieces(near_hbm, near, 10 + PIECES)
+
     in_f[me] = out_f[me]
     pair_loads = pltpu.make_async_remote_copy(
         src_ref=loads_hbm,

time: 15.8 us -> 15.5 us (0.981)
  Pallas kernels: 15 us -> 14.7 us
    pallas_call x1, Pallas kernels: 13.9 us -> 13.6 us  [on_device(): pl.pallas_call(functools.partial(kernel, dims), out_shape=(pltpu.VMEM(ful...]
where the time goes in v6:
time: 15.5 us; the launch traced here: 15.4 us
  Pallas kernels  14.7 us (95%)
  between operations  0.64 us (4%)
    pallas_call x1, Pallas kernels, on_device(): pl.pallas_call(functools.partial(kernel, dims), out_shape=(pltpu.VMEM(ful...  13.6 us
    pallas_call x1, Pallas kernels, on_device(): pl.pallas_call(finish, out_shape=(full, full), in_specs=[vmem] * 4, out_s...  1.11 us

profile of v6, /device:TPU:0, one launch (start us, length us, event | category | flops | bytes accessed | tf_op | source)
XLA Modules:
  0.0 15.4 jit_solution(1945049414121211323)
XLA Ops:
  0.6 13.6 %hierarchical.1 = (bf16[16,128,128]{2,1,0:T(8,128)(2,1)S(1)}, f32[16,128,128]{2,1,0:T(8,128)S(1)}, bf16[16,32,128]{2,1,0:T(8,128)(2,1)S(1)}, bf16[16,32,128]{2,1,0:T(8,128)(2,1)S(1)}) custom-call(bf16[16,128,128]{2,1,0:T(8,128)(2,1)} %charges_hbm.1, bf16[16,128,128]{2,1,0:T(8,128)(2,1)} %loads_hbm.1, bf16[16,32,128]{2,1,0:T(8,128)(2,1)} %bases_hbm.1, ...), custom_call_target="tpu_custom_call" | custom-call | tf_op jit(solution)/shard_map/hierarchical/pallas_call | solution.py:401
  14.3 1.1 %finish.1 = (bf16[16,128,128]{2,1,0:T(8,128)(2,1)}, bf16[16,128,128]{2,1,0:T(8,128)(2,1)}) custom-call(bf16[16,128,128]{2,1,0:T(8,128)(2,1)S(1)} %get-tuple-element.6.potentials, f32[16,128,128]{2,1,0:T(8,128)S(1)} %get-tuple-element.7.near_adj, bf16[16,32,128]{2,1,0:T(8,128)(2,1)S(1)} %get-tuple-element.8.far_adj, ...), custom_call_target="tpu_custom_call" | custom-call | tf_op jit(solution)/shard_map/finish/pallas_call | solution.py:452

commit v7 on v6

--- a/solution.py
+++ b/solution.py
@@ -224,19 +224,9 @@
     get_far_slots = fetch(far_slots_hbm, far_slots, 6)
     get_rows = fetch(near_rows_hbm, near_rows, 7)
     get_cols = fetch(near_cols_hbm, near_cols, 8)
-    get_near = fetch_pieces(near_hbm, near, 10 + PIECES)
+    get_near = [fetch(near_hbm, near, 10 + PIECES)]
 
     in_f[me] = out_f[me]
-    pair_loads = pltpu.make_async_remote_copy(
-        src_ref=loads_hbm,
-        dst_ref=all_loads.at[pl.ds(core * clusters, clusters)],
-        send_sem=pair_send.at[0],
-        recv_sem=pair_recv.at[0],
-        device_id={"sub": other},
-        device_id_type=MESH,
-    )
-    pair_loads.start()
-
     get_loads.wait()
     bases32[...] = bases[...].astype(f32).reshape(clusters * rank, block)
     for c in range(clusters):
@@ -279,6 +269,15 @@
 
     loop(chunks, merge)
     loop(peers - 1, lambda step: far_copy(out_r, in_r, r_send, r_recv, step).start())
+    pair_loads = pltpu.make_async_remote_copy(
+        src_ref=loads_hbm,
+        dst_ref=all_loads.at[pl.ds(core * clusters, clusters)],
+        send_sem=pair_send.at[0],
+        recv_sem=pair_recv.at[0],
+        device_id={"sub": other},
+        device_id_type=MESH,
+    )
+    pair_loads.start()
     in_r[me] = out_r[me]
 
     get_rows.wait()

time: 15.5 us -> 15.5 us (level)
  no operation moved by 1% of the time
where the time goes in v7:
time: 15.5 us; the launch traced here: 15.4 us
  Pallas kernels  14.7 us (95%)
  between operations  0.64 us (4%)
    pallas_call x1, Pallas kernels, on_device(): pl.pallas_call(functools.partial(kernel, dims), out_shape=(pltpu.VMEM(ful...  13.6 us
    pallas_call x1, Pallas kernels, on_device(): pl.pallas_call(finish, out_shape=(full, full), in_specs=[vmem] * 4, out_s...  1.11 us

profile of v7, /device:TPU:0, one launch (start us, length us, event | category | flops | bytes accessed | tf_op | source)
XLA Modules:
  0.0 15.4 jit_solution(354937010233064869)
XLA Ops:
  0.6 13.6 %hierarchical.1 = (bf16[16,128,128]{2,1,0:T(8,128)(2,1)S(1)}, f32[16,128,128]{2,1,0:T(8,128)S(1)}, bf16[16,32,128]{2,1,0:T(8,128)(2,1)S(1)}, bf16[16,32,128]{2,1,0:T(8,128)(2,1)S(1)}) custom-call(bf16[16,128,128]{2,1,0:T(8,128)(2,1)} %charges_hbm.1, bf16[16,128,128]{2,1,0:T(8,128)(2,1)} %loads_hbm.1, bf16[16,32,128]{2,1,0:T(8,128)(2,1)} %bases_hbm.1, ...), custom_call_target="tpu_custom_call" | custom-call | tf_op jit(solution)/shard_map/hierarchical/pallas_call | solution.py:400
  14.3 1.1 %finish.1 = (bf16[16,128,128]{2,1,0:T(8,128)(2,1)}, bf16[16,128,128]{2,1,0:T(8,128)(2,1)}) custom-call(bf16[16,128,128]{2,1,0:T(8,128)(2,1)S(1)} %get-tuple-element.6.potentials, f32[16,128,128]{2,1,0:T(8,128)S(1)} %get-tuple-element.7.near_adj, bf16[16,32,128]{2,1,0:T(8,128)(2,1)S(1)} %get-tuple-element.8.far_adj, ...), custom_call_target="tpu_custom_call" | custom-call | tf_op jit(solution)/shard_map/finish/pallas_call | solution.py:451
